TPU v7x, 32 devices: a whole 2x2x4 slice. The times are simulated.
32 devices in a mesh: lon: 8 (over z, y), bin: 4 (over x, core).
Axes of the slice: x: 2, y: 2, z: 4, core: 2. Of those that a mesh axis runs over, the one named last changes fastest.
Arguments:
- adjoint_start: float32 [8, 4, 8, 1024], P('bin', None, None, 'lon'), may hold values from -6 to 6
- base_flux: float32 [8, 8, 1024], P('bin', None, 'lon'), may hold values from 0.1 to 1
- vertical_mixing: float32 [3, 8, 1024], P(None, None, 'lon'), may hold values from 0.05 to 5
- zonal_fraction: float32 [4, 8], replicated, may hold values from 0.02 to 0.98
- meridional_fraction: float32 [4], replicated, may hold values from 0.05 to 0.95
- zonal_hops: int32 [8], replicated, may hold values from -3 to 3, as said below
- cell_shift: int32 [8], replicated, may hold values from 0 to 127, as said below
Outputs:
- adjoint_end: float32 [8, 4, 8, 1024], P('bin', None, None, 'lon')
- emission_gradient: float32 [8, 1024], P(None, 'lon')
Inputs may be any that keep to these rules, and one draw needn't show every extreme that they name: For every h from 1 to 3, exactly (3 - h + 1) * 1 rows have zonal_hops >= h and exactly as many have zonal_hops <= -h. `cell_shift`: both extreme values occur.
All inputs are finite; a program needn't handle non-finite values.
Results may differ from a plain program's by a relative error of at most 0.0001.
Values sent between devices are 32-bit elements; how exact they have to be, the bound alone decides.
A program may use at most 64 MiB of HBM per device.

v0:
```python
import jax
import jax.numpy as jnp
from jax import lax
from jax.sharding import PartitionSpec as P

HMAX = 3
STEPS = 2
right_face = (0.0, -1.0, 7.0, 7.0, -1.0)
slope_face = (1.0, -8.0, 0.0, 8.0, -1.0)
curve_face = (3.0, -18.0, 30.0, -18.0, 3.0)


def padded_2(block, sides, width):
    for axis, dim in sides:
        count = lax.axis_size(axis)
        forward = [(i, i + 1) for i in range(count - 1)]
        forward.append((count - 1, 0))
        backward = [(target, source) for source, target in forward]
        low = lax.ppermute(
            lax.slice_in_dim(block, block.shape[dim] - width, None, axis=dim), axis, forward
        )
        high = lax.ppermute(lax.slice_in_dim(block, 0, width, axis=dim), axis, backward)
        block = jnp.concatenate([low, block, high], axis=dim)
    return block


def from_behind(value, axis, by):
    length = lax.axis_size(axis)
    return lax.ppermute(value, axis, [(i, (i + by) % length) for i in range(length)])


def flux_weights(courant):
    square = courant * courant
    cubic_part = 0.5 * square * (1.0 - courant * (2.0 / 3.0))
    return [
        (
            courant * right_face[offset]
            - 0.5 * square * slope_face[offset]
            + cubic_part * curve_face[offset]
        )
        / 12.0
        for offset in range(5)
    ]


def vertical_solve(adjoint_field, vertical_mixing):
    levels = adjoint_field.shape[1]
    ratios = []
    values = []
    for layer_index in range(levels):
        pivot_value = 1.0
        source_row = adjoint_field[:, layer_index]
        if layer_index < levels - 1:
            pivot_value = pivot_value + vertical_mixing[layer_index]
        if layer_index > 0:
            below = vertical_mixing[layer_index - 1]
            pivot_value = pivot_value + below + below * ratios[-1]
            source_row = source_row + below * values[-1]
        values.append(source_row / pivot_value)
        if layer_index < levels - 1:
            ratios.append(-vertical_mixing[layer_index] / pivot_value)
    solved = [values[levels - 1]]
    for layer_index in range(levels - 2, -1, -1):
        solved.insert(0, values[layer_index] - ratios[layer_index] * solved[0])
    return jnp.stack(solved, axis=1)


def zonal_adjoint(adjoint_field, zonal_fraction):
    sector_width = adjoint_field.shape[3]
    weights = flux_weights(zonal_fraction)
    padded = padded_2(adjoint_field, (("lon", 3),), 3)
    face_flux = 0.0
    for offset in range(5):
        start_col = 3 - (offset - 2)
        face_flux = (
            face_flux
            + weights[offset][:, :, None]
            * padded[:, :, :, start_col : start_col + sector_width + 1]
        )
    return adjoint_field - face_flux[:, :, :, :sector_width] + face_flux[:, :, :, 1:]


def roll_rows(field_data, offsets):
    width = field_data.shape[3]
    bit_count = max(1, (width - 1).bit_length())
    for bit_index in range(bit_count):
        amount = 1 << bit_index
        moved = jnp.roll(field_data, -amount, axis=3)
        chosen = (offsets // amount % 2)[None, None, :, None] == 1
        field_data = jnp.where(chosen, moved, field_data)
    return field_data


def pick_cells(adjoint_field, following, cell_shift):
    sector_width = adjoint_field.shape[3]
    joined = jnp.concatenate([adjoint_field, following], axis=3)
    return roll_rows(joined, cell_shift)[:, :, :, :sector_width]


def hop_shift(adjoint_field, zonal_hops, cell_shift):
    following = from_behind(adjoint_field, "lon", -1)
    picked = pick_cells(adjoint_field, following, cell_shift)
    hop_rows = zonal_hops[None, None, :, None]
    eastern = jnp.where(hop_rows > 0, picked, 0.0)
    western = jnp.where(hop_rows < 0, picked, 0.0)
    result_field = jnp.where(hop_rows == 0, picked, 0.0)
    for hop_count in range(1, HMAX + 1):
        eastern = from_behind(eastern, "lon", -1)
        western = from_behind(western, "lon", 1)
        result_field = result_field + jnp.where(hop_rows == hop_count, eastern, 0.0)
        result_field = result_field + jnp.where(hop_rows == -hop_count, western, 0.0)
    return result_field


def meridional_adjoint(adjoint_field, meridional_fraction):
    lat_count = adjoint_field.shape[2]
    weights = flux_weights(meridional_fraction)
    padded = jnp.pad(adjoint_field, ((0, 0), (0, 0), (3, 3), (0, 0)))
    face_flux = 0.0
    for offset in range(5):
        start_row = 3 - (offset - 2)
        face_flux = (
            face_flux
            + weights[offset][:, None, None] * padded[:, :, start_row : start_row + lat_count + 1]
        )
    return adjoint_field - face_flux[:, :, :lat_count] + face_flux[:, :, 1:]


def per_device(
    adjoint_start,
    base_flux,
    vertical_mixing,
    zonal_fraction,
    meridional_fraction,
    zonal_hops,
    cell_shift,
):
    adjoint_field = adjoint_start
    gradient_sum = jnp.zeros(base_flux.shape[1:], jnp.float32)
    for step_index in range(STEPS):
        adjoint_field = vertical_solve(adjoint_field, vertical_mixing)
        adjoint_field = zonal_adjoint(adjoint_field, zonal_fraction)
        adjoint_field = hop_shift(adjoint_field, zonal_hops, cell_shift)
        adjoint_field = meridional_adjoint(adjoint_field, meridional_fraction)
        local_term = jnp.sum(base_flux * adjoint_field[:, 0], axis=0)
        gradient_sum = gradient_sum + lax.psum(local_term, "bin")
    return (adjoint_field, gradient_sum)


def solution(mesh):
    return jax.shard_map(
        per_device,
        mesh=mesh,
        in_specs=(
            P("bin", None, None, "lon"),
            P("bin", None, "lon"),
            P(None, None, "lon"),
            P(),
            P(),
            P(),
            P(),
        ),
        out_specs=(P("bin", None, None, "lon"), P(None, "lon")),
        check_vma=False,
    )
```

profile of v0, /device:TPU:0, one launch (start us, length us, event | category | flops | bytes accessed | tf_op | source)
XLA Modules:
  0.0 83.2 jit_solution(6797585602489341325)
XLA Ops:
  0.6 0.8 fusion.54
  1.4 0.7 copy-done.2
  2.3 6.0 %collective-permute-start = (f32[2,4,8,3]{3,2,1,0:T(8,128)S(1)}, f32[2,4,8,3]{3,2,1,0:T(8,128)S(1)}, u32[]{:S(2)}, u32[]{:S(2)}) collective-permute-start(f32[2,4,8,3]{3,2,1,0:T(8,128)S(1)} %get-tuple-element.30), channel_id=1, source_target_pairs={{4,0},{8,4},{12,8},{16,12},{20,16},{24,20},{28,24},{0,28},{5,1},{9... | collective-permute-start | bytes 2312 | tf_op jit(solution)/shard_map/ppermute | solution.py:22
  8.3 0.6 copy-done.5
  9.0 0.9 %collective-permute-done = f32[2,4,8,3]{3,2,1,0:T(8,128)S(1)} collective-permute-done((f32[2,4,8,3]{3,2,1,0:T(8,128)S(1)}, f32[2,4,8,3]{3,2,1,0:T(8,128)S(1)}, u32[]{:S(2)}, u32[]{:S(2)}) %collective-permute-start) | collective-permute-done | bytes 800 | tf_op jit(solution)/shard_map/ppermute | solution.py:22
  9.9 5.0 %collective-permute-done.1 = f32[2,4,8,3]{3,2,1,0:T(8,128)S(1)} collective-permute-done((f32[2,4,8,3]{3,2,1,0:T(8,128)S(1)}, f32[2,4,8,3]{3,2,1,0:T(8,128)S(1)}, u32[]{:S(2)}, u32[]{:S(2)}) %collective-permute-start.1) | collective-permute-done | bytes 800 | tf_op jit(solution)/shard_map/ppermute | solution.py:19
  15.0 0.2 fusion.26
  15.3 0.6 copy-done.6
  15.9 3.3 %collective-permute-done.2 = f32[2,4,8,128]{3,2,1,0:T(8,128)S(1)} collective-permute-done((f32[2,4,8,128]{3,2,1,0:T(8,128)S(1)}, f32[2,4,8,128]{3,2,1,0:T(8,128)S(1)}, u32[]{:S(2)}, u32[]{:S(2)}) %collective-permute-start.2) | collective-permute-done | bytes 32800 | tf_op jit(solution)/shard_map/ppermute | solution.py:29
  19.2 0.1 fusion.2
  19.3 0.1 fusion.3
  19.5 0.1 maximum_select_fusion
  19.6 0.1 maximum_select_fusion.1
  19.8 0.1 maximum_select_fusion.2
  20.0 0.1 maximum_select_fusion.3
  20.2 0.1 maximum_select_fusion.4
  20.4 0.1 maximum_select_fusion.5
  20.6 4.7 %collective-permute-start.3 = (f32[2,4,8,128]{3,2,1,0:T(8,128)S(1)}, f32[2,4,8,128]{3,2,1,0:T(8,128)S(1)}, u32[]{:S(2)}, u32[]{:S(2)}) collective-permute-start(f32[2,4,8,128]{3,2,1,0:T(8,128)S(1)} %get-tuple-element.10), channel_id=1, source_target_pairs={{0,28},{4,0},{8,4},{12,8},{16,12},{20,16},{24,20},{28,24},{1,29},{... | collective-permute-start | bytes 98312 | tf_op jit(solution)/shard_map/ppermute | solution.py:29
  25.4 1.9 %collective-permute-done.4 = f32[2,4,8,128]{3,2,1,0:T(8,128)S(1)} collective-permute-done((f32[2,4,8,128]{3,2,1,0:T(8,128)S(1)}, f32[2,4,8,128]{3,2,1,0:T(8,128)S(1)}, u32[]{:S(2)}, u32[]{:S(2)}) %collective-permute-start.4) | collective-permute-done | bytes 32800 | tf_op jit(solution)/shard_map/ppermute | solution.py:29
  27.2 4.8 %collective-permute-start.5 = (f32[2,4,8,128]{3,2,1,0:T(8,128)S(1)}, f32[2,4,8,128]{3,2,1,0:T(8,128)S(1)}, u32[]{:S(2)}, u32[]{:S(2)}) collective-permute-start(f32[2,4,8,128]{3,2,1,0:T(8,128)S(1)} %collective-permute-done.3), channel_id=1, source_target_pairs={{0,28},{4,0},{8,4},{12,8},{16,12},{20,16},{24,20},{28,24},{1,29},{... | collective-permute-start | bytes 98312 | tf_op jit(solution)/shard_map/ppermute | solution.py:29
  32.1 1.8 %collective-permute-done.6 = f32[2,4,8,128]{3,2,1,0:T(8,128)S(1)} collective-permute-done((f32[2,4,8,128]{3,2,1,0:T(8,128)S(1)}, f32[2,4,8,128]{3,2,1,0:T(8,128)S(1)}, u32[]{:S(2)}, u32[]{:S(2)}) %collective-permute-start.6) | collective-permute-done | bytes 32800 | tf_op jit(solution)/shard_map/ppermute | solution.py:29
  33.9 5.0 %collective-permute-start.7 = (f32[2,4,8,128]{3,2,1,0:T(8,128)S(1)}, f32[2,4,8,128]{3,2,1,0:T(8,128)S(1)}, u32[]{:S(2)}, u32[]{:S(2)}) collective-permute-start(f32[2,4,8,128]{3,2,1,0:T(8,128)S(1)} %collective-permute-done.5), channel_id=1, source_target_pairs={{0,28},{4,0},{8,4},{12,8},{16,12},{20,16},{24,20},{28,24},{1,29},{... | collective-permute-start | bytes 98312 | tf_op jit(solution)/shard_map/ppermute | solution.py:29
  38.8 2.0 %collective-permute-done.8 = f32[2,4,8,128]{3,2,1,0:T(8,128)S(1)} collective-permute-done((f32[2,4,8,128]{3,2,1,0:T(8,128)S(1)}, f32[2,4,8,128]{3,2,1,0:T(8,128)S(1)}, u32[]{:S(2)}, u32[]{:S(2)}) %collective-permute-start.8) | collective-permute-done | bytes 32800 | tf_op jit(solution)/shard_map/ppermute | solution.py:29
  40.8 0.1 select_add_fusion.1
  40.9 0.1 fusion.8
  41.1 4.7 %collective-permute-start.9 = (f32[2,4,8,3]{3,2,1,0:T(8,128)S(1)}, f32[2,4,8,3]{3,2,1,0:T(8,128)S(1)}, u32[]{:S(2)}, u32[]{:S(2)}) collective-permute-start(f32[2,4,8,3]{3,2,1,0:T(8,128)S(1)} %get-tuple-element.26), channel_id=1, source_target_pairs={{4,0},{8,4},{12,8},{16,12},{20,16},{24,20},{28,24},{0,28},{5,1},{9... | collective-permute-start | bytes 2312 | tf_op jit(solution)/shard_map/ppermute | solution.py:22
  45.9 1.9 %collective-permute-done.10 = f32[2,4,8,3]{3,2,1,0:T(8,128)S(1)} collective-permute-done((f32[2,4,8,3]{3,2,1,0:T(8,128)S(1)}, f32[2,4,8,3]{3,2,1,0:T(8,128)S(1)}, u32[]{:S(2)}, u32[]{:S(2)}) %collective-permute-start.10) | collective-permute-done | bytes 800 | tf_op jit(solution)/shard_map/ppermute | solution.py:19
  47.8 0.2 fusion.22
  48.1 4.7 %collective-permute-start.11 = (f32[2,4,8,128]{3,2,1,0:T(8,128)S(1)}, f32[2,4,8,128]{3,2,1,0:T(8,128)S(1)}, u32[]{:S(2)}, u32[]{:S(2)}) collective-permute-start(f32[2,4,8,128]{3,2,1,0:T(8,128)S(1)} %slice_add_fusion.1), channel_id=1, source_target_pairs={{0,28},{4,0},{8,4},{12,8},{16,12},{20,16},{24,20},{28,24},{1,29},{... | collective-permute-start | bytes 98312 | tf_op jit(solution)/shard_map/ppermute | solution.py:29
  52.8 1.6 %collective-permute-done.11 = f32[2,4,8,128]{3,2,1,0:T(8,128)S(1)} collective-permute-done((f32[2,4,8,128]{3,2,1,0:T(8,128)S(1)}, f32[2,4,8,128]{3,2,1,0:T(8,128)S(1)}, u32[]{:S(2)}, u32[]{:S(2)}) %collective-permute-start.11) | collective-permute-done | bytes 32800 | tf_op jit(solution)/shard_map/ppermute | solution.py:29
  54.4 0.1 fusion
  54.5 0.1 fusion.1
  54.7 0.1 maximum_select_fusion.6
  54.9 0.1 maximum_select_fusion.7
  55.0 0.1 maximum_select_fusion.8
  55.2 0.1 maximum_select_fusion.9
  55.4 0.1 maximum_select_fusion.10
  55.6 0.1 maximum_select_fusion.11
  55.9 5.1 %collective-permute-start.12 = (f32[2,4,8,128]{3,2,1,0:T(8,128)S(1)}, f32[2,4,8,128]{3,2,1,0:T(8,128)S(1)}, u32[]{:S(2)}, u32[]{:S(2)}) collective-permute-start(f32[2,4,8,128]{3,2,1,0:T(8,128)S(1)} %get-tuple-element.4), channel_id=1, source_target_pairs={{0,28},{4,0},{8,4},{12,8},{16,12},{20,16},{24,20},{28,24},{1,29},{... | collective-permute-start | bytes 98312 | tf_op jit(solution)/shard_map/ppermute | solution.py:29
  60.9 1.8 %collective-permute-done.13 = f32[2,4,8,128]{3,2,1,0:T(8,128)S(1)} collective-permute-done((f32[2,4,8,128]{3,2,1,0:T(8,128)S(1)}, f32[2,4,8,128]{3,2,1,0:T(8,128)S(1)}, u32[]{:S(2)}, u32[]{:S(2)}) %collective-permute-start.13) | collective-permute-done | bytes 32800 | tf_op jit(solution)/shard_map/ppermute | solution.py:29
  62.8 4.8 %collective-permute-start.14 = (f32[2,4,8,128]{3,2,1,0:T(8,128)S(1)}, f32[2,4,8,128]{3,2,1,0:T(8,128)S(1)}, u32[]{:S(2)}, u32[]{:S(2)}) collective-permute-start(f32[2,4,8,128]{3,2,1,0:T(8,128)S(1)} %collective-permute-done.12), channel_id=1, source_target_pairs={{0,28},{4,0},{8,4},{12,8},{16,12},{20,16},{24,20},{28,24},{1,29},{... | collective-permute-start | bytes 98312 | tf_op jit(solution)/shard_map/ppermute | solution.py:29
  67.5 1.8 %collective-permute-done.15 = f32[2,4,8,128]{3,2,1,0:T(8,128)S(1)} collective-permute-done((f32[2,4,8,128]{3,2,1,0:T(8,128)S(1)}, f32[2,4,8,128]{3,2,1,0:T(8,128)S(1)}, u32[]{:S(2)}, u32[]{:S(2)}) %collective-permute-start.15) | collective-permute-done | bytes 32800 | tf_op jit(solution)/shard_map/ppermute | solution.py:29
  69.4 4.8 %collective-permute-start.16 = (f32[2,4,8,128]{3,2,1,0:T(8,128)S(1)}, f32[2,4,8,128]{3,2,1,0:T(8,128)S(1)}, u32[]{:S(2)}, u32[]{:S(2)}) collective-permute-start(f32[2,4,8,128]{3,2,1,0:T(8,128)S(1)} %collective-permute-done.14), channel_id=1, source_target_pairs={{0,28},{4,0},{8,4},{12,8},{16,12},{20,16},{24,20},{28,24},{1,29},{... | collective-permute-start | bytes 98312 | tf_op jit(solution)/shard_map/ppermute | solution.py:29
  74.2 1.8 %collective-permute-done.17 = f32[2,4,8,128]{3,2,1,0:T(8,128)S(1)} collective-permute-done((f32[2,4,8,128]{3,2,1,0:T(8,128)S(1)}, f32[2,4,8,128]{3,2,1,0:T(8,128)S(1)}, u32[]{:S(2)}, u32[]{:S(2)}) %collective-permute-start.17) | collective-permute-done | bytes 32800 | tf_op jit(solution)/shard_map/ppermute | solution.py:29
  76.0 0.1 select_add_fusion
  76.1 0.1 fusion.17
  76.2 0.7 copy-done.3
  76.9 6.3 %psum.16 = f32[8,128]{1,0:T(8,128)} all-reduce(f32[8,128]{1,0:T(8,128)S(1)} %add.377), channel_id=1, replica_groups=mesh['lon'=8,'bin'=4] {'bin'}, use_global_device_ids=true, to_apply=%region_1.2 | all-reduce | flops 1024 | bytes 8192 | tf_op jit(solution)/shard_map/psum | solution.py:146
  (80 shorter events, 2.0 us)
Async XLA Ops:
  0.6 0.8 copy-start
  1.4 0.8 copy-start.2
  2.3 6.0 %copy-start.4 = (f32[4,8]{1,0:T(4,128)S(1)}, f32[4,8]{1,0:T(4,128)}, u32[]{:S(2)}) copy-start(f32[4,8]{1,0:T(4,128)} %param.10) | copy-start | bytes 388
  2.3 7.6 %collective-permute-start = (f32[2,4,8,3]{3,2,1,0:T(8,128)S(1)}, f32[2,4,8,3]{3,2,1,0:T(8,128)S(1)}, u32[]{:S(2)}, u32[]{:S(2)}) collective-permute-start(f32[2,4,8,3]{3,2,1,0:T(8,128)S(1)} %get-tuple-element.30), channel_id=1, source_target_pairs={{4,0},{8,4},{12,8},{16,12},{20,16},{24,20},{28,24},{0,28},{5,1},{9... | collective-permute-start | bytes 2312 | tf_op jit(solution)/shard_map/ppermute | solution.py:22
  8.3 0.7 copy-start.5
  8.3 6.6 %collective-permute-start.1 = (f32[2,4,8,3]{3,2,1,0:T(8,128)S(1)}, f32[2,4,8,3]{3,2,1,0:T(8,128)S(1)}, u32[]{:S(2)}, u32[]{:S(2)}) collective-permute-start(f32[2,4,8,3]{3,2,1,0:T(8,128)S(1)} %get-tuple-element.31), channel_id=1, source_target_pairs={{0,4},{4,8},{8,12},{12,16},{16,20},{20,24},{24,28},{28,0},{1,5},{5... | collective-permute-start | bytes 2312 | tf_op jit(solution)/shard_map/ppermute | solution.py:19
  15.2 0.7 copy-start.6
  15.3 3.9 %collective-permute-start.2 = (f32[2,4,8,128]{3,2,1,0:T(8,128)S(1)}, f32[2,4,8,128]{3,2,1,0:T(8,128)S(1)}, u32[]{:S(2)}, u32[]{:S(2)}) collective-permute-start(f32[2,4,8,128]{3,2,1,0:T(8,128)S(1)} %slice_add_fusion.3), channel_id=1, source_target_pairs={{0,28},{4,0},{8,4},{12,8},{16,12},{20,16},{24,20},{28,24},{1,29},{... | collective-permute-start | bytes 98312 | tf_op jit(solution)/shard_map/ppermute | solution.py:29
  20.6 18.2 %copy-start.7 = (f32[4]{0:T(128)S(1)}, f32[4]{0:T(128)}, u32[]{:S(2)}) copy-start(f32[4]{0:T(128)} %param.11) | copy-start | bytes 52
  20.6 6.6 %collective-permute-start.4 = (f32[2,4,8,128]{3,2,1,0:T(8,128)S(1)}, f32[2,4,8,128]{3,2,1,0:T(8,128)S(1)}, u32[]{:S(2)}, u32[]{:S(2)}) collective-permute-start(f32[2,4,8,128]{3,2,1,0:T(8,128)S(1)} %broadcast_select_fusion.1), channel_id=1, source_target_pairs={{0,4},{4,8},{8,12},{12,16},{16,20},{20,24},{24,28},{28,0},{1,5},{5... | collective-permute-start | bytes 98312 | tf_op jit(solution)/shard_map/ppermute | solution.py:29
  20.6 6.6 %collective-permute-start.3 = (f32[2,4,8,128]{3,2,1,0:T(8,128)S(1)}, f32[2,4,8,128]{3,2,1,0:T(8,128)S(1)}, u32[]{:S(2)}, u32[]{:S(2)}) collective-permute-start(f32[2,4,8,128]{3,2,1,0:T(8,128)S(1)} %get-tuple-element.10), channel_id=1, source_target_pairs={{0,28},{4,0},{8,4},{12,8},{16,12},{20,16},{24,20},{28,24},{1,29},{... | collective-permute-start | bytes 98312 | tf_op jit(solution)/shard_map/ppermute | solution.py:29
  27.2 6.6 %collective-permute-start.6 = (f32[2,4,8,128]{3,2,1,0:T(8,128)S(1)}, f32[2,4,8,128]{3,2,1,0:T(8,128)S(1)}, u32[]{:S(2)}, u32[]{:S(2)}) collective-permute-start(f32[2,4,8,128]{3,2,1,0:T(8,128)S(1)} %collective-permute-done.4), channel_id=1, source_target_pairs={{0,4},{4,8},{8,12},{12,16},{16,20},{20,24},{24,28},{28,0},{1,5},{5... | collective-permute-start | bytes 98312 | tf_op jit(solution)/shard_map/ppermute | solution.py:29
  27.2 6.6 %collective-permute-start.5 = (f32[2,4,8,128]{3,2,1,0:T(8,128)S(1)}, f32[2,4,8,128]{3,2,1,0:T(8,128)S(1)}, u32[]{:S(2)}, u32[]{:S(2)}) collective-permute-start(f32[2,4,8,128]{3,2,1,0:T(8,128)S(1)} %collective-permute-done.3), channel_id=1, source_target_pairs={{0,28},{4,0},{8,4},{12,8},{16,12},{20,16},{24,20},{28,24},{1,29},{... | collective-permute-start | bytes 98312 | tf_op jit(solution)/shard_map/ppermute | solution.py:29
  33.9 6.9 %collective-permute-start.8 = (f32[2,4,8,128]{3,2,1,0:T(8,128)S(1)}, f32[2,4,8,128]{3,2,1,0:T(8,128)S(1)}, u32[]{:S(2)}, u32[]{:S(2)}) collective-permute-start(f32[2,4,8,128]{3,2,1,0:T(8,128)S(1)} %collective-permute-done.6), channel_id=1, source_target_pairs={{0,4},{4,8},{8,12},{12,16},{16,20},{20,24},{24,28},{28,0},{1,5},{5... | collective-permute-start | bytes 98312 | tf_op jit(solution)/shard_map/ppermute | solution.py:29
  33.9 6.9 %collective-permute-start.7 = (f32[2,4,8,128]{3,2,1,0:T(8,128)S(1)}, f32[2,4,8,128]{3,2,1,0:T(8,128)S(1)}, u32[]{:S(2)}, u32[]{:S(2)}) collective-permute-start(f32[2,4,8,128]{3,2,1,0:T(8,128)S(1)} %collective-permute-done.5), channel_id=1, source_target_pairs={{0,28},{4,0},{8,4},{12,8},{16,12},{20,16},{24,20},{28,24},{1,29},{... | collective-permute-start | bytes 98312 | tf_op jit(solution)/shard_map/ppermute | solution.py:29
  41.1 6.6 %collective-permute-start.10 = (f32[2,4,8,3]{3,2,1,0:T(8,128)S(1)}, f32[2,4,8,3]{3,2,1,0:T(8,128)S(1)}, u32[]{:S(2)}, u32[]{:S(2)}) collective-permute-start(f32[2,4,8,3]{3,2,1,0:T(8,128)S(1)} %get-tuple-element.27), channel_id=1, source_target_pairs={{0,4},{4,8},{8,12},{12,16},{16,20},{20,24},{24,28},{28,0},{1,5},{5... | collective-permute-start | bytes 2312 | tf_op jit(solution)/shard_map/ppermute | solution.py:19
  41.1 6.6 %collective-permute-start.9 = (f32[2,4,8,3]{3,2,1,0:T(8,128)S(1)}, f32[2,4,8,3]{3,2,1,0:T(8,128)S(1)}, u32[]{:S(2)}, u32[]{:S(2)}) collective-permute-start(f32[2,4,8,3]{3,2,1,0:T(8,128)S(1)} %get-tuple-element.26), channel_id=1, source_target_pairs={{4,0},{8,4},{12,8},{16,12},{20,16},{24,20},{28,24},{0,28},{5,1},{9... | collective-permute-start | bytes 2312 | tf_op jit(solution)/shard_map/ppermute | solution.py:22
  48.1 6.3 %collective-permute-start.11 = (f32[2,4,8,128]{3,2,1,0:T(8,128)S(1)}, f32[2,4,8,128]{3,2,1,0:T(8,128)S(1)}, u32[]{:S(2)}, u32[]{:S(2)}) collective-permute-start(f32[2,4,8,128]{3,2,1,0:T(8,128)S(1)} %slice_add_fusion.1), channel_id=1, source_target_pairs={{0,28},{4,0},{8,4},{12,8},{16,12},{20,16},{24,20},{28,24},{1,29},{... | collective-permute-start | bytes 98312 | tf_op jit(solution)/shard_map/ppermute | solution.py:29
  55.9 6.9 %collective-permute-start.13 = (f32[2,4,8,128]{3,2,1,0:T(8,128)S(1)}, f32[2,4,8,128]{3,2,1,0:T(8,128)S(1)}, u32[]{:S(2)}, u32[]{:S(2)}) collective-permute-start(f32[2,4,8,128]{3,2,1,0:T(8,128)S(1)} %broadcast_select_fusion), channel_id=1, source_target_pairs={{0,4},{4,8},{8,12},{12,16},{16,20},{20,24},{24,28},{28,0},{1,5},{5... | collective-permute-start | bytes 98312 | tf_op jit(solution)/shard_map/ppermute | solution.py:29
  55.9 6.9 %collective-permute-start.12 = (f32[2,4,8,128]{3,2,1,0:T(8,128)S(1)}, f32[2,4,8,128]{3,2,1,0:T(8,128)S(1)}, u32[]{:S(2)}, u32[]{:S(2)}) collective-permute-start(f32[2,4,8,128]{3,2,1,0:T(8,128)S(1)} %get-tuple-element.4), channel_id=1, source_target_pairs={{0,28},{4,0},{8,4},{12,8},{16,12},{20,16},{24,20},{28,24},{1,29},{... | collective-permute-start | bytes 98312 | tf_op jit(solution)/shard_map/ppermute | solution.py:29
  62.8 6.6 %collective-permute-start.15 = (f32[2,4,8,128]{3,2,1,0:T(8,128)S(1)}, f32[2,4,8,128]{3,2,1,0:T(8,128)S(1)}, u32[]{:S(2)}, u32[]{:S(2)}) collective-permute-start(f32[2,4,8,128]{3,2,1,0:T(8,128)S(1)} %collective-permute-done.13), channel_id=1, source_target_pairs={{0,4},{4,8},{8,12},{12,16},{16,20},{20,24},{24,28},{28,0},{1,5},{5... | collective-permute-start | bytes 98312 | tf_op jit(solution)/shard_map/ppermute | solution.py:29
  62.8 6.6 %collective-permute-start.14 = (f32[2,4,8,128]{3,2,1,0:T(8,128)S(1)}, f32[2,4,8,128]{3,2,1,0:T(8,128)S(1)}, u32[]{:S(2)}, u32[]{:S(2)}) collective-permute-start(f32[2,4,8,128]{3,2,1,0:T(8,128)S(1)} %collective-permute-done.12), channel_id=1, source_target_pairs={{0,28},{4,0},{8,4},{12,8},{16,12},{20,16},{24,20},{28,24},{1,29},{... | collective-permute-start | bytes 98312 | tf_op jit(solution)/shard_map/ppermute | solution.py:29
  69.4 6.6 %collective-permute-start.17 = (f32[2,4,8,128]{3,2,1,0:T(8,128)S(1)}, f32[2,4,8,128]{3,2,1,0:T(8,128)S(1)}, u32[]{:S(2)}, u32[]{:S(2)}) collective-permute-start(f32[2,4,8,128]{3,2,1,0:T(8,128)S(1)} %collective-permute-done.15), channel_id=1, source_target_pairs={{0,4},{4,8},{8,12},{12,16},{16,20},{20,24},{24,28},{28,0},{1,5},{5... | collective-permute-start | bytes 98312 | tf_op jit(solution)/shard_map/ppermute | solution.py:29
  69.4 6.6 %collective-permute-start.16 = (f32[2,4,8,128]{3,2,1,0:T(8,128)S(1)}, f32[2,4,8,128]{3,2,1,0:T(8,128)S(1)}, u32[]{:S(2)}, u32[]{:S(2)}) collective-permute-start(f32[2,4,8,128]{3,2,1,0:T(8,128)S(1)} %collective-permute-done.14), channel_id=1, source_target_pairs={{0,28},{4,0},{8,4},{12,8},{16,12},{20,16},{24,20},{28,24},{1,29},{... | collective-permute-start | bytes 98312 | tf_op jit(solution)/shard_map/ppermute | solution.py:29
  76.2 0.7 copy-start.3
  76.9 6.3 %copy-start.1 = (f32[2,4,8,128]{3,2,1,0:T(8,128)}, f32[2,4,8,128]{3,2,1,0:T(8,128)S(1)}, u32[]{:S(2)}) copy-start(f32[2,4,8,128]{3,2,1,0:T(8,128)S(1)} %slice_add_fusion) | copy-start | bytes 98308
where the time goes:
time: 83.5 us; the launch traced here: 83.2 us
  starting transfers between devices  44.6 us (53%)
  waiting for transfers between devices  23.9 us (29%)
  blocking collectives  6.26 us (7%)
  local copies, waits for them, and re-layouts  3.77 us (5%)
  other arithmetic  3.62 us (4%)
  between operations  1.04 us (1%)
    ppermute x14, starting transfers between devices, from_behind(): lax.ppermute(value, axis, [(i, (i + by) % length) for i in range(length)])  33.8 us
    ppermute x14, waiting for transfers between devices, from_behind(): lax.ppermute(value, axis, [(i, (i + by) % length) for i in range(length)])  16.1 us
    ppermute x2, starting transfers between devices, padded_2(): lax.ppermute(lax.slice_in_dim(block, 0, width, axis=dim), axis, backward)  10.7 us
    ppermute x2, waiting for transfers between devices, padded_2(): lax.ppermute(lax.slice_in_dim(block, block.shape[dim] - width, None, axis...  6.9 us
    psum x1, blocking collectives, per_device(): gradient_sum = gradient_sum + lax.psum(local_term, 'bin')  6.26 us
    unnamed x16, local copies, waits for them, and re-layouts  2.61 us
  transfers between devices with their start and end apart: 18, of which 11 were waited for; matrix products, arithmetic and copies ran while one was open for 0% of the time, Pallas kernels for 0%

commit v1 on v0

--- a/solution.py
+++ b/solution.py
@@ -143,7 +143,7 @@
         adjoint_field = hop_shift(adjoint_field, zonal_hops, cell_shift)
         adjoint_field = meridional_adjoint(adjoint_field, meridional_fraction)
         local_term = jnp.sum(base_flux * adjoint_field[:, 0], axis=0)
-        gradient_sum = gradient_sum + lax.psum(local_term, "bin")
+        gradient_sum = gradient_sum + jnp.sum(lax.all_gather(local_term, "bin"), axis=0)
     return (adjoint_field, gradient_sum)
 
 

time: 83.5 us -> 88.2 us (1.056)
  blocking collectives: 6.26 us -> 10.4 us
    all_gather x0 -> x2, blocking collectives: none -> 10.4 us  [per_device(): lax.all_gather(local_term, 'bin')]
    psum x1 -> x0, blocking collectives: 6.26 us -> none  [per_device(): gradient_sum = gradient_sum + lax.psum(local_term, 'bin')]
where the time goes in v1:
time: 88.2 us; the launch traced here: 87.9 us
  starting transfers between devices  44.6 us (51%)
  waiting for transfers between devices  23.9 us (27%)
  blocking collectives  10.4 us (12%)
  other arithmetic  4.22 us (5%)
  local copies, waits for them, and re-layouts  3.77 us (4%)
  between operations  1.04 us (1%)
    ppermute x14, starting transfers between devices, from_behind(): lax.ppermute(value, axis, [(i, (i + by) % length) for i in range(length)])  33.8 us
    ppermute x14, waiting for transfers between devices, from_behind(): lax.ppermute(value, axis, [(i, (i + by) % length) for i in range(length)])  16.1 us
    ppermute x2, starting transfers between devices, padded_2(): lax.ppermute(lax.slice_in_dim(block, 0, width, axis=dim), axis, backward)  10.7 us
    all_gather x2, blocking collectives, per_device(): lax.all_gather(local_term, 'bin')  10.4 us
    ppermute x2, waiting for transfers between devices, padded_2(): lax.ppermute(lax.slice_in_dim(block, block.shape[dim] - width, None, axis...  6.9 us
    unnamed x16, local copies, waits for them, and re-layouts  2.61 us
  transfers between devices with their start and end apart: 18, of which 11 were waited for; matrix products, arithmetic and copies ran while one was open for 0% of the time, Pallas kernels for 0%

profile of v1, /device:TPU:0, one launch (start us, length us, event | category | flops | bytes accessed | tf_op | source)
XLA Modules:
  0.0 87.9 jit_solution(13490388088320036954)
XLA Ops:
  0.6 0.8 fusion.54
  1.4 0.7 copy-done.2
  2.3 6.0 %collective-permute-start = (f32[2,4,8,3]{3,2,1,0:T(8,128)S(1)}, f32[2,4,8,3]{3,2,1,0:T(8,128)S(1)}, u32[]{:S(2)}, u32[]{:S(2)}) collective-permute-start(f32[2,4,8,3]{3,2,1,0:T(8,128)S(1)} %get-tuple-element.30), channel_id=1, source_target_pairs={{4,0},{8,4},{12,8},{16,12},{20,16},{24,20},{28,24},{0,28},{5,1},{9... | collective-permute-start | bytes 2312 | tf_op jit(solution)/shard_map/ppermute | solution.py:22
  8.3 0.6 copy-done.5
  9.0 0.9 %collective-permute-done = f32[2,4,8,3]{3,2,1,0:T(8,128)S(1)} collective-permute-done((f32[2,4,8,3]{3,2,1,0:T(8,128)S(1)}, f32[2,4,8,3]{3,2,1,0:T(8,128)S(1)}, u32[]{:S(2)}, u32[]{:S(2)}) %collective-permute-start) | collective-permute-done | bytes 800 | tf_op jit(solution)/shard_map/ppermute | solution.py:22
  9.9 5.0 %collective-permute-done.1 = f32[2,4,8,3]{3,2,1,0:T(8,128)S(1)} collective-permute-done((f32[2,4,8,3]{3,2,1,0:T(8,128)S(1)}, f32[2,4,8,3]{3,2,1,0:T(8,128)S(1)}, u32[]{:S(2)}, u32[]{:S(2)}) %collective-permute-start.1) | collective-permute-done | bytes 800 | tf_op jit(solution)/shard_map/ppermute | solution.py:19
  15.0 0.2 fusion.26
  15.3 0.6 copy-done.6
  15.9 3.3 %collective-permute-done.2 = f32[2,4,8,128]{3,2,1,0:T(8,128)S(1)} collective-permute-done((f32[2,4,8,128]{3,2,1,0:T(8,128)S(1)}, f32[2,4,8,128]{3,2,1,0:T(8,128)S(1)}, u32[]{:S(2)}, u32[]{:S(2)}) %collective-permute-start.2) | collective-permute-done | bytes 32800 | tf_op jit(solution)/shard_map/ppermute | solution.py:29
  19.2 0.1 fusion.2
  19.3 0.1 fusion.3
  19.5 0.1 maximum_select_fusion
  19.6 0.1 maximum_select_fusion.1
  20.0 0.1 maximum_select_fusion.3
  20.4 0.1 maximum_select_fusion.5
  20.6 4.7 %collective-permute-start.3 = (f32[2,4,8,128]{3,2,1,0:T(8,128)S(1)}, f32[2,4,8,128]{3,2,1,0:T(8,128)S(1)}, u32[]{:S(2)}, u32[]{:S(2)}) collective-permute-start(f32[2,4,8,128]{3,2,1,0:T(8,128)S(1)} %get-tuple-element.10), channel_id=1, source_target_pairs={{0,28},{4,0},{8,4},{12,8},{16,12},{20,16},{24,20},{28,24},{1,29},{... | collective-permute-start | bytes 98312 | tf_op jit(solution)/shard_map/ppermute | solution.py:29
  25.4 1.9 %collective-permute-done.4 = f32[2,4,8,128]{3,2,1,0:T(8,128)S(1)} collective-permute-done((f32[2,4,8,128]{3,2,1,0:T(8,128)S(1)}, f32[2,4,8,128]{3,2,1,0:T(8,128)S(1)}, u32[]{:S(2)}, u32[]{:S(2)}) %collective-permute-start.4) | collective-permute-done | bytes 32800 | tf_op jit(solution)/shard_map/ppermute | solution.py:29
  27.2 4.8 %collective-permute-start.5 = (f32[2,4,8,128]{3,2,1,0:T(8,128)S(1)}, f32[2,4,8,128]{3,2,1,0:T(8,128)S(1)}, u32[]{:S(2)}, u32[]{:S(2)}) collective-permute-start(f32[2,4,8,128]{3,2,1,0:T(8,128)S(1)} %collective-permute-done.3), channel_id=1, source_target_pairs={{0,28},{4,0},{8,4},{12,8},{16,12},{20,16},{24,20},{28,24},{1,29},{... | collective-permute-start | bytes 98312 | tf_op jit(solution)/shard_map/ppermute | solution.py:29
  32.1 1.8 %collective-permute-done.6 = f32[2,4,8,128]{3,2,1,0:T(8,128)S(1)} collective-permute-done((f32[2,4,8,128]{3,2,1,0:T(8,128)S(1)}, f32[2,4,8,128]{3,2,1,0:T(8,128)S(1)}, u32[]{:S(2)}, u32[]{:S(2)}) %collective-permute-start.6) | collective-permute-done | bytes 32800 | tf_op jit(solution)/shard_map/ppermute | solution.py:29
  33.9 5.0 %collective-permute-start.7 = (f32[2,4,8,128]{3,2,1,0:T(8,128)S(1)}, f32[2,4,8,128]{3,2,1,0:T(8,128)S(1)}, u32[]{:S(2)}, u32[]{:S(2)}) collective-permute-start(f32[2,4,8,128]{3,2,1,0:T(8,128)S(1)} %collective-permute-done.5), channel_id=1, source_target_pairs={{0,28},{4,0},{8,4},{12,8},{16,12},{20,16},{24,20},{28,24},{1,29},{... | collective-permute-start | bytes 98312 | tf_op jit(solution)/shard_map/ppermute | solution.py:29
  38.8 2.0 %collective-permute-done.8 = f32[2,4,8,128]{3,2,1,0:T(8,128)S(1)} collective-permute-done((f32[2,4,8,128]{3,2,1,0:T(8,128)S(1)}, f32[2,4,8,128]{3,2,1,0:T(8,128)S(1)}, u32[]{:S(2)}, u32[]{:S(2)}) %collective-permute-start.8) | collective-permute-done | bytes 32800 | tf_op jit(solution)/shard_map/ppermute | solution.py:29
  40.8 0.1 select_add_fusion.1
  40.9 0.1 fusion.8
  41.1 4.7 %collective-permute-start.9 = (f32[2,4,8,3]{3,2,1,0:T(8,128)S(1)}, f32[2,4,8,3]{3,2,1,0:T(8,128)S(1)}, u32[]{:S(2)}, u32[]{:S(2)}) collective-permute-start(f32[2,4,8,3]{3,2,1,0:T(8,128)S(1)} %get-tuple-element.26), channel_id=1, source_target_pairs={{4,0},{8,4},{12,8},{16,12},{20,16},{24,20},{28,24},{0,28},{5,1},{9... | collective-permute-start | bytes 2312 | tf_op jit(solution)/shard_map/ppermute | solution.py:22
  45.9 1.9 %collective-permute-done.10 = f32[2,4,8,3]{3,2,1,0:T(8,128)S(1)} collective-permute-done((f32[2,4,8,3]{3,2,1,0:T(8,128)S(1)}, f32[2,4,8,3]{3,2,1,0:T(8,128)S(1)}, u32[]{:S(2)}, u32[]{:S(2)}) %collective-permute-start.10) | collective-permute-done | bytes 800 | tf_op jit(solution)/shard_map/ppermute | solution.py:19
  47.8 0.2 fusion.22
  48.1 4.7 %collective-permute-start.11 = (f32[2,4,8,128]{3,2,1,0:T(8,128)S(1)}, f32[2,4,8,128]{3,2,1,0:T(8,128)S(1)}, u32[]{:S(2)}, u32[]{:S(2)}) collective-permute-start(f32[2,4,8,128]{3,2,1,0:T(8,128)S(1)} %slice_add_fusion.1), channel_id=1, source_target_pairs={{0,28},{4,0},{8,4},{12,8},{16,12},{20,16},{24,20},{28,24},{1,29},{... | collective-permute-start | bytes 98312 | tf_op jit(solution)/shard_map/ppermute | solution.py:29
  52.8 1.6 %collective-permute-done.11 = f32[2,4,8,128]{3,2,1,0:T(8,128)S(1)} collective-permute-done((f32[2,4,8,128]{3,2,1,0:T(8,128)S(1)}, f32[2,4,8,128]{3,2,1,0:T(8,128)S(1)}, u32[]{:S(2)}, u32[]{:S(2)}) %collective-permute-start.11) | collective-permute-done | bytes 32800 | tf_op jit(solution)/shard_map/ppermute | solution.py:29
  54.4 0.1 fusion
  54.5 0.1 fusion.1
  54.7 0.1 maximum_select_fusion.6
  54.9 0.1 maximum_select_fusion.7
  55.0 0.1 maximum_select_fusion.8
  55.2 0.1 maximum_select_fusion.9
  55.4 0.1 maximum_select_fusion.10
  55.6 0.1 maximum_select_fusion.11
  55.9 5.1 %collective-permute-start.12 = (f32[2,4,8,128]{3,2,1,0:T(8,128)S(1)}, f32[2,4,8,128]{3,2,1,0:T(8,128)S(1)}, u32[]{:S(2)}, u32[]{:S(2)}) collective-permute-start(f32[2,4,8,128]{3,2,1,0:T(8,128)S(1)} %get-tuple-element.4), channel_id=1, source_target_pairs={{0,28},{4,0},{8,4},{12,8},{16,12},{20,16},{24,20},{28,24},{1,29},{... | collective-permute-start | bytes 98312 | tf_op jit(solution)/shard_map/ppermute | solution.py:29
  60.9 1.8 %collective-permute-done.13 = f32[2,4,8,128]{3,2,1,0:T(8,128)S(1)} collective-permute-done((f32[2,4,8,128]{3,2,1,0:T(8,128)S(1)}, f32[2,4,8,128]{3,2,1,0:T(8,128)S(1)}, u32[]{:S(2)}, u32[]{:S(2)}) %collective-permute-start.13) | collective-permute-done | bytes 32800 | tf_op jit(solution)/shard_map/ppermute | solution.py:29
  62.8 4.8 %collective-permute-start.14 = (f32[2,4,8,128]{3,2,1,0:T(8,128)S(1)}, f32[2,4,8,128]{3,2,1,0:T(8,128)S(1)}, u32[]{:S(2)}, u32[]{:S(2)}) collective-permute-start(f32[2,4,8,128]{3,2,1,0:T(8,128)S(1)} %collective-permute-done.12), channel_id=1, source_target_pairs={{0,28},{4,0},{8,4},{12,8},{16,12},{20,16},{24,20},{28,24},{1,29},{... | collective-permute-start | bytes 98312 | tf_op jit(solution)/shard_map/ppermute | solution.py:29
  67.5 1.8 %collective-permute-done.15 = f32[2,4,8,128]{3,2,1,0:T(8,128)S(1)} collective-permute-done((f32[2,4,8,128]{3,2,1,0:T(8,128)S(1)}, f32[2,4,8,128]{3,2,1,0:T(8,128)S(1)}, u32[]{:S(2)}, u32[]{:S(2)}) %collective-permute-start.15) | collective-permute-done | bytes 32800 | tf_op jit(solution)/shard_map/ppermute | solution.py:29
  69.4 4.8 %collective-permute-start.16 = (f32[2,4,8,128]{3,2,1,0:T(8,128)S(1)}, f32[2,4,8,128]{3,2,1,0:T(8,128)S(1)}, u32[]{:S(2)}, u32[]{:S(2)}) collective-permute-start(f32[2,4,8,128]{3,2,1,0:T(8,128)S(1)} %collective-permute-done.14), channel_id=1, source_target_pairs={{0,28},{4,0},{8,4},{12,8},{16,12},{20,16},{24,20},{28,24},{1,29},{... | collective-permute-start | bytes 98312 | tf_op jit(solution)/shard_map/ppermute | solution.py:29
  74.2 1.8 %collective-permute-done.17 = f32[2,4,8,128]{3,2,1,0:T(8,128)S(1)} collective-permute-done((f32[2,4,8,128]{3,2,1,0:T(8,128)S(1)}, f32[2,4,8,128]{3,2,1,0:T(8,128)S(1)}, u32[]{:S(2)}, u32[]{:S(2)}) %collective-permute-start.17) | collective-permute-done | bytes 32800 | tf_op jit(solution)/shard_map/ppermute | solution.py:29
  76.0 0.1 select_add_fusion
  76.1 0.1 fusion.17
  76.2 0.7 copy-done.3
  76.9 5.2 %all-gather.1 = f32[32,128]{1,0:T(8,128)S(1)} all-gather(f32[8,128]{1,0:T(8,128)S(1)} %get-tuple-element.2), channel_id=3, replica_groups=mesh['lon'=8,'bin'=4] {'bin'}, dimensions={0}, use_global_device_ids=true | all-gather | bytes 20480 | tf_op jit(solution)/shard_map/all_gather | solution.py:146
  82.1 5.2 %all-gather = f32[32,128]{1,0:T(8,128)S(1)} all-gather(f32[8,128]{1,0:T(8,128)S(1)} %get-tuple-element.3), channel_id=2, replica_groups=mesh['lon'=8,'bin'=4] {'bin'}, dimensions={0}, use_global_device_ids=true | all-gather | bytes 20480 | tf_op jit(solution)/shard_map/all_gather | solution.py:146
  87.3 0.6 add.373
  (83 shorter events, 2.2 us)
Async XLA Ops:
  0.6 0.8 copy-start
  1.4 0.8 copy-start.2
  2.3 6.0 %copy-start.4 = (f32[4,8]{1,0:T(4,128)S(1)}, f32[4,8]{1,0:T(4,128)}, u32[]{:S(2)}) copy-start(f32[4,8]{1,0:T(4,128)} %param.10) | copy-start | bytes 388
  2.3 7.6 %collective-permute-start = (f32[2,4,8,3]{3,2,1,0:T(8,128)S(1)}, f32[2,4,8,3]{3,2,1,0:T(8,128)S(1)}, u32[]{:S(2)}, u32[]{:S(2)}) collective-permute-start(f32[2,4,8,3]{3,2,1,0:T(8,128)S(1)} %get-tuple-element.30), channel_id=1, source_target_pairs={{4,0},{8,4},{12,8},{16,12},{20,16},{24,20},{28,24},{0,28},{5,1},{9... | collective-permute-start | bytes 2312 | tf_op jit(solution)/shard_map/ppermute | solution.py:22
  8.3 0.7 copy-start.5
  8.3 6.6 %collective-permute-start.1 = (f32[2,4,8,3]{3,2,1,0:T(8,128)S(1)}, f32[2,4,8,3]{3,2,1,0:T(8,128)S(1)}, u32[]{:S(2)}, u32[]{:S(2)}) collective-permute-start(f32[2,4,8,3]{3,2,1,0:T(8,128)S(1)} %get-tuple-element.31), channel_id=1, source_target_pairs={{0,4},{4,8},{8,12},{12,16},{16,20},{20,24},{24,28},{28,0},{1,5},{5... | collective-permute-start | bytes 2312 | tf_op jit(solution)/shard_map/ppermute | solution.py:19
  15.2 0.7 copy-start.6
  15.3 3.9 %collective-permute-start.2 = (f32[2,4,8,128]{3,2,1,0:T(8,128)S(1)}, f32[2,4,8,128]{3,2,1,0:T(8,128)S(1)}, u32[]{:S(2)}, u32[]{:S(2)}) collective-permute-start(f32[2,4,8,128]{3,2,1,0:T(8,128)S(1)} %slice_add_fusion.3), channel_id=1, source_target_pairs={{0,28},{4,0},{8,4},{12,8},{16,12},{20,16},{24,20},{28,24},{1,29},{... | collective-permute-start | bytes 98312 | tf_op jit(solution)/shard_map/ppermute | solution.py:29
  20.6 18.2 %copy-start.7 = (f32[4]{0:T(128)S(1)}, f32[4]{0:T(128)}, u32[]{:S(2)}) copy-start(f32[4]{0:T(128)} %param.11) | copy-start | bytes 52
  20.6 6.6 %collective-permute-start.4 = (f32[2,4,8,128]{3,2,1,0:T(8,128)S(1)}, f32[2,4,8,128]{3,2,1,0:T(8,128)S(1)}, u32[]{:S(2)}, u32[]{:S(2)}) collective-permute-start(f32[2,4,8,128]{3,2,1,0:T(8,128)S(1)} %broadcast_select_fusion.1), channel_id=1, source_target_pairs={{0,4},{4,8},{8,12},{12,16},{16,20},{20,24},{24,28},{28,0},{1,5},{5... | collective-permute-start | bytes 98312 | tf_op jit(solution)/shard_map/ppermute | solution.py:29
  20.6 6.6 %collective-permute-start.3 = (f32[2,4,8,128]{3,2,1,0:T(8,128)S(1)}, f32[2,4,8,128]{3,2,1,0:T(8,128)S(1)}, u32[]{:S(2)}, u32[]{:S(2)}) collective-permute-start(f32[2,4,8,128]{3,2,1,0:T(8,128)S(1)} %get-tuple-element.10), channel_id=1, source_target_pairs={{0,28},{4,0},{8,4},{12,8},{16,12},{20,16},{24,20},{28,24},{1,29},{... | collective-permute-start | bytes 98312 | tf_op jit(solution)/shard_map/ppermute | solution.py:29
  27.2 6.6 %collective-permute-start.6 = (f32[2,4,8,128]{3,2,1,0:T(8,128)S(1)}, f32[2,4,8,128]{3,2,1,0:T(8,128)S(1)}, u32[]{:S(2)}, u32[]{:S(2)}) collective-permute-start(f32[2,4,8,128]{3,2,1,0:T(8,128)S(1)} %collective-permute-done.4), channel_id=1, source_target_pairs={{0,4},{4,8},{8,12},{12,16},{16,20},{20,24},{24,28},{28,0},{1,5},{5... | collective-permute-start | bytes 98312 | tf_op jit(solution)/shard_map/ppermute | solution.py:29
  27.2 6.6 %collective-permute-start.5 = (f32[2,4,8,128]{3,2,1,0:T(8,128)S(1)}, f32[2,4,8,128]{3,2,1,0:T(8,128)S(1)}, u32[]{:S(2)}, u32[]{:S(2)}) collective-permute-start(f32[2,4,8,128]{3,2,1,0:T(8,128)S(1)} %collective-permute-done.3), channel_id=1, source_target_pairs={{0,28},{4,0},{8,4},{12,8},{16,12},{20,16},{24,20},{28,24},{1,29},{... | collective-permute-start | bytes 98312 | tf_op jit(solution)/shard_map/ppermute | solution.py:29
  33.9 6.9 %collective-permute-start.8 = (f32[2,4,8,128]{3,2,1,0:T(8,128)S(1)}, f32[2,4,8,128]{3,2,1,0:T(8,128)S(1)}, u32[]{:S(2)}, u32[]{:S(2)}) collective-permute-start(f32[2,4,8,128]{3,2,1,0:T(8,128)S(1)} %collective-permute-done.6), channel_id=1, source_target_pairs={{0,4},{4,8},{8,12},{12,16},{16,20},{20,24},{24,28},{28,0},{1,5},{5... | collective-permute-start | bytes 98312 | tf_op jit(solution)/shard_map/ppermute | solution.py:29
  33.9 6.9 %collective-permute-start.7 = (f32[2,4,8,128]{3,2,1,0:T(8,128)S(1)}, f32[2,4,8,128]{3,2,1,0:T(8,128)S(1)}, u32[]{:S(2)}, u32[]{:S(2)}) collective-permute-start(f32[2,4,8,128]{3,2,1,0:T(8,128)S(1)} %collective-permute-done.5), channel_id=1, source_target_pairs={{0,28},{4,0},{8,4},{12,8},{16,12},{20,16},{24,20},{28,24},{1,29},{... | collective-permute-start | bytes 98312 | tf_op jit(solution)/shard_map/ppermute | solution.py:29
  41.1 6.6 %collective-permute-start.10 = (f32[2,4,8,3]{3,2,1,0:T(8,128)S(1)}, f32[2,4,8,3]{3,2,1,0:T(8,128)S(1)}, u32[]{:S(2)}, u32[]{:S(2)}) collective-permute-start(f32[2,4,8,3]{3,2,1,0:T(8,128)S(1)} %get-tuple-element.27), channel_id=1, source_target_pairs={{0,4},{4,8},{8,12},{12,16},{16,20},{20,24},{24,28},{28,0},{1,5},{5... | collective-permute-start | bytes 2312 | tf_op jit(solution)/shard_map/ppermute | solution.py:19
  41.1 6.6 %collective-permute-start.9 = (f32[2,4,8,3]{3,2,1,0:T(8,128)S(1)}, f32[2,4,8,3]{3,2,1,0:T(8,128)S(1)}, u32[]{:S(2)}, u32[]{:S(2)}) collective-permute-start(f32[2,4,8,3]{3,2,1,0:T(8,128)S(1)} %get-tuple-element.26), channel_id=1, source_target_pairs={{4,0},{8,4},{12,8},{16,12},{20,16},{24,20},{28,24},{0,28},{5,1},{9... | collective-permute-start | bytes 2312 | tf_op jit(solution)/shard_map/ppermute | solution.py:22
  48.1 6.3 %collective-permute-start.11 = (f32[2,4,8,128]{3,2,1,0:T(8,128)S(1)}, f32[2,4,8,128]{3,2,1,0:T(8,128)S(1)}, u32[]{:S(2)}, u32[]{:S(2)}) collective-permute-start(f32[2,4,8,128]{3,2,1,0:T(8,128)S(1)} %slice_add_fusion.1), channel_id=1, source_target_pairs={{0,28},{4,0},{8,4},{12,8},{16,12},{20,16},{24,20},{28,24},{1,29},{... | collective-permute-start | bytes 98312 | tf_op jit(solution)/shard_map/ppermute | solution.py:29
  55.9 6.9 %collective-permute-start.13 = (f32[2,4,8,128]{3,2,1,0:T(8,128)S(1)}, f32[2,4,8,128]{3,2,1,0:T(8,128)S(1)}, u32[]{:S(2)}, u32[]{:S(2)}) collective-permute-start(f32[2,4,8,128]{3,2,1,0:T(8,128)S(1)} %broadcast_select_fusion), channel_id=1, source_target_pairs={{0,4},{4,8},{8,12},{12,16},{16,20},{20,24},{24,28},{28,0},{1,5},{5... | collective-permute-start | bytes 98312 | tf_op jit(solution)/shard_map/ppermute | solution.py:29
  55.9 6.9 %collective-permute-start.12 = (f32[2,4,8,128]{3,2,1,0:T(8,128)S(1)}, f32[2,4,8,128]{3,2,1,0:T(8,128)S(1)}, u32[]{:S(2)}, u32[]{:S(2)}) collective-permute-start(f32[2,4,8,128]{3,2,1,0:T(8,128)S(1)} %get-tuple-element.4), channel_id=1, source_target_pairs={{0,28},{4,0},{8,4},{12,8},{16,12},{20,16},{24,20},{28,24},{1,29},{... | collective-permute-start | bytes 98312 | tf_op jit(solution)/shard_map/ppermute | solution.py:29
  62.8 6.6 %collective-permute-start.15 = (f32[2,4,8,128]{3,2,1,0:T(8,128)S(1)}, f32[2,4,8,128]{3,2,1,0:T(8,128)S(1)}, u32[]{:S(2)}, u32[]{:S(2)}) collective-permute-start(f32[2,4,8,128]{3,2,1,0:T(8,128)S(1)} %collective-permute-done.13), channel_id=1, source_target_pairs={{0,4},{4,8},{8,12},{12,16},{16,20},{20,24},{24,28},{28,0},{1,5},{5... | collective-permute-start | bytes 98312 | tf_op jit(solution)/shard_map/ppermute | solution.py:29
  62.8 6.6 %collective-permute-start.14 = (f32[2,4,8,128]{3,2,1,0:T(8,128)S(1)}, f32[2,4,8,128]{3,2,1,0:T(8,128)S(1)}, u32[]{:S(2)}, u32[]{:S(2)}) collective-permute-start(f32[2,4,8,128]{3,2,1,0:T(8,128)S(1)} %collective-permute-done.12), channel_id=1, source_target_pairs={{0,28},{4,0},{8,4},{12,8},{16,12},{20,16},{24,20},{28,24},{1,29},{... | collective-permute-start | bytes 98312 | tf_op jit(solution)/shard_map/ppermute | solution.py:29
  69.4 6.6 %collective-permute-start.17 = (f32[2,4,8,128]{3,2,1,0:T(8,128)S(1)}, f32[2,4,8,128]{3,2,1,0:T(8,128)S(1)}, u32[]{:S(2)}, u32[]{:S(2)}) collective-permute-start(f32[2,4,8,128]{3,2,1,0:T(8,128)S(1)} %collective-permute-done.15), channel_id=1, source_target_pairs={{0,4},{4,8},{8,12},{12,16},{16,20},{20,24},{24,28},{28,0},{1,5},{5... | collective-permute-start | bytes 98312 | tf_op jit(solution)/shard_map/ppermute | solution.py:29
  69.4 6.6 %collective-permute-start.16 = (f32[2,4,8,128]{3,2,1,0:T(8,128)S(1)}, f32[2,4,8,128]{3,2,1,0:T(8,128)S(1)}, u32[]{:S(2)}, u32[]{:S(2)}) collective-permute-start(f32[2,4,8,128]{3,2,1,0:T(8,128)S(1)} %collective-permute-done.14), channel_id=1, source_target_pairs={{0,28},{4,0},{8,4},{12,8},{16,12},{20,16},{24,20},{28,24},{1,29},{... | collective-permute-start | bytes 98312 | tf_op jit(solution)/shard_map/ppermute | solution.py:29
  76.2 0.7 copy-start.3
  76.9 5.2 %copy-start.1 = (f32[2,4,8,128]{3,2,1,0:T(8,128)}, f32[2,4,8,128]{3,2,1,0:T(8,128)S(1)}, u32[]{:S(2)}) copy-start(f32[2,4,8,128]{3,2,1,0:T(8,128)S(1)} %slice_add_fusion) | copy-start | bytes 98308
